TPU v7x, 128 devices: a whole 4x4x4 slice. The times are simulated.
128 devices in a mesh: leaf: 8 (over z, x_hi), grid: 16 (over y, x_lo, core).
Axes of the slice: x: 4 (x_hi: 2, x_lo: 2; x = x_hi * 2 + x_lo), y: 4, z: 4, core: 2. Of those that a mesh axis runs over, the one named last changes fastest.
Arguments:
- root_inverse: float32 [4096, 4096], P('grid', 'leaf'), may hold values from -1 to 12, as said below
- middle_inverse: float32 [2048, 4096], P('grid', 'leaf'), may hold values from -1 to 12, as said below
- middle_panel: float32 [4096, 4096], P('grid', 'leaf'), may hold values from -0.1875 to 0.1875
- lower_root: float32 [4096, 8192], P('grid', 'leaf'), may hold values from -0.1875 to 0.1875
- lower_middle: float32 [2048, 8192], P(None, 'leaf'), may hold values from -0.25 to 0.25
- block_pattern: int32 [4, 32], replicated, may hold values 0 or 1
- lower_diagonal: float32 [8192], P('leaf'), may hold values from 1.5 to 6
Outputs:
- middle_cross: float32 [4096, 4096], P('grid', 'leaf')
- middle_variance: float32 [4096], P('leaf')
- lower_cross: float32 [4096, 8192], P('grid', 'leaf')
- lower_parent: float32 [2048, 8192], P('grid', 'leaf')
- lower_variance: float32 [8192], P('leaf')
Inputs may be any that keep to these rules, and one draw needn't show every extreme that they name: `root_inverse`: symmetric; its diagonal entries lie between 1.5 and 12. `middle_inverse`: each front's 2048 x 2048 block is symmetric; its diagonal entries lie between 1.5 and 12.
All inputs are finite; a program needn't handle non-finite values.
Results may differ from a plain program's by a relative error of at most 0.0001.
Values sent between devices are 32-bit elements; how exact they have to be, the bound alone decides.
A program may use at most 128 MiB of HBM per device.

v0:
```python
import jax
import jax.numpy as jnp
from jax import lax
from jax.sharding import PartitionSpec as P

S1 = 2048
BLK = 128


exact = lax.Precision.HIGHEST


def root_times(panel, root_rows):
    return lax.psum_scatter(
        lax.dot_general(
            root_rows,
            panel,
            (((0,), (0,)), ((), ())),
            precision=exact,
            preferred_element_type=jnp.float32,
        ),
        "grid",
        scatter_dimension=0,
        tiled=True,
    )


def local(
    root_inverse,
    middle_inverse,
    middle_panel,
    lower_root,
    lower_middle,
    block_pattern,
    lower_diagonal,
):
    leaf_count = lax.axis_size("leaf")
    leaf_index = lax.axis_index("leaf")
    grid_index = lax.axis_index("grid")
    parent_front = leaf_index // (leaf_count // 2)
    child_front = leaf_index // (leaf_count // 4)
    root_rows, middle_rows, middle_block = (
        lax.all_gather(root_inverse, "leaf", axis=1, tiled=True),
        lax.all_gather(middle_panel, "leaf", axis=1, tiled=True),
        lax.all_gather(middle_inverse, "leaf", axis=1, tiled=True),
    )
    middle_rows = lax.dynamic_slice_in_dim(middle_rows, parent_front * S1, S1, 1)
    middle_block = lax.dynamic_slice_in_dim(middle_block, parent_front * S1, S1, 1)
    local_rows = lower_root.shape[0]
    blocks_here = local_rows // BLK
    pattern = lax.dynamic_slice(
        block_pattern, (child_front, grid_index * blocks_here), (1, blocks_here)
    )
    keep = jnp.repeat(pattern[0].astype(jnp.float32), BLK)
    lower_panel = lower_root * keep[:, None]
    first_side = root_times(middle_panel, root_rows)
    reduced = lower_panel - jnp.dot(
        middle_rows, lower_middle, precision=exact, preferred_element_type=jnp.float32
    )
    root_side = root_times(reduced, root_rows)
    parent_own = jnp.dot(
        middle_block, lower_middle, precision=exact, preferred_element_type=jnp.float32
    )
    middle_count = middle_inverse.shape[0]
    parent_side = parent_own - lax.psum_scatter(
        lax.dot_general(
            middle_rows,
            root_side,
            (((0,), (0,)), ((), ())),
            precision=exact,
            preferred_element_type=jnp.float32,
        ),
        "grid",
        scatter_dimension=0,
        tiled=True,
    )
    own_columns = middle_inverse.shape[1]
    global_rows = grid_index * middle_count + jnp.arange(middle_count, dtype=jnp.int32)
    global_columns = leaf_index % (leaf_count // 2) * own_columns + jnp.arange(
        own_columns, dtype=jnp.int32
    )
    on_diagonal = global_rows[:, None] == global_columns[None, :]
    middle_part = jnp.sum(jnp.where(on_diagonal, middle_inverse, 0.0), axis=0) + jnp.sum(
        middle_panel * first_side, axis=0
    )
    lower_rows = lax.dynamic_slice_in_dim(lower_middle, grid_index * middle_count, middle_count, 0)
    lower_part = jnp.sum(lower_panel * root_side, axis=0) + jnp.sum(
        lower_rows * parent_side, axis=0
    )
    middle_total, lower_total = lax.psum((middle_part, lower_part), "grid")
    return (-first_side, middle_total, -root_side, -parent_side, lower_diagonal + lower_total)


def solution(mesh):
    in_specs = (
        P("grid", "leaf"),
        P("grid", "leaf"),
        P("grid", "leaf"),
        P("grid", "leaf"),
        P(None, "leaf"),
        P(),
        P("leaf"),
    )
    out_specs = (P("grid", "leaf"), P("leaf"), P("grid", "leaf"), P("grid", "leaf"), P("leaf"))
    return jax.shard_map(local, mesh=mesh, in_specs=in_specs, out_specs=out_specs, check_vma=False)
```

profile of v0, /device:TPU:1, one launch (start us, length us, event | category | flops | bytes accessed | tf_op | source)
XLA Modules:
  0.0 651.1 jit_solution(7684410831926605279)
XLA Ops:
  7.2 0.0 all-gather.6.cloned.1.call-start
  7.2 0.7 all-gather.6.cloned.1.call-update
  7.9 0.0 all-gather.4.cloned.1.call-start
  7.9 0.7 all-gather.4.cloned.1.call-update
  8.6 0.0 reduce-scatter.6.cloned.1.call-start
  8.7 1.6 copy.12
  10.3 0.8 convert_bitcast_fusion
  11.1 0.1 broadcast_bitcast_fusion
  11.1 73.6 %all-gather.6.cloned.1.call-done = f32[256,4096]{1,0:T(8,128)} async-done(((f32[256,512]{1,0:T(8,128)}), f32[256,4096]{1,0:T(8,128)}) %all-gather.6.cloned.1.call-update) | async-done | bytes 4194320 | tf_op jit(solution)/shard_map/all_gather | solution.py:44
  84.7 16.2 %fusion.4 = f32[256,1024]{0,1:T(8,128)S(1)} fusion(f32[2048,1024]{1,0:T(8,128)} %param.11, f32[256,4096]{1,0:T(8,128)} %all-gather.6.cloned.1.call-done, s32[]{:T(128)S(6)} %select_n.37, f32[256,1024]{0,1:T(8,128)S(1)} %copy.12, f32[256]{0:T(256)S(1)} %broadcast_bitcast_fusion), kind=kOutput, calls=%fused_computation.5 | convolution fusion | flops 6442975232 | bytes 12583940 | tf_op jit(solution)/shard_map/dot_general | solution.py:57
  101.0 55.4 %all-gather.4.cloned.1.call-done = f32[256,4096]{1,0:T(8,128)} async-done(((f32[256,512]{1,0:T(8,128)}), f32[256,4096]{1,0:T(8,128)}) %all-gather.4.cloned.1.call-update) | async-done | bytes 4194320 | tf_op jit(solution)/shard_map/all_gather | solution.py:43
  156.4 17.2 %convolution_bitcast_fusion = f32[4096,1024]{0,1:T(8,128)} fusion(f32[256,1024]{0,1:T(8,128)S(1)} %fusion.4, f32[256,4096]{1,0:T(8,128)} %all-gather.4.cloned.1.call-done), kind=kOutput, calls=%fused_computation | convolution fusion | flops 12884901888 | bytes 22020096 | tf_op jit(solution)/shard_map/dot_general | solution.py:15
  173.6 0.0 reduce-scatter.6.cloned.1.call-update
  173.7 0.2 reduce-scatter.4.cloned.1.call-start
  173.9 0.8 copy-done
  174.7 10.5 %fusion.13 = f32[4096,512]{1,0:T(8,128)} fusion(f32[256,4096]{1,0:T(8,128)} %all-gather.4.cloned.1.call-done, f32[256,512]{1,0:T(8,128)S(1)} %copy-done), kind=kOutput, calls=%fused_computation.21 | convolution fusion | flops 6442450944 | bytes 13107200 | tf_op jit(solution)/shard_map/dot_general | solution.py:15
  185.2 0.0 all-gather.8.cloned.1.call-start
  185.3 0.5 all-gather.8.cloned.1.call-update
  185.8 0.0 reduce-scatter.8.cloned.1.call-start
  185.8 166.8 %reduce-scatter.6.cloned.1.call-done = f32[256,1024]{0,1:T(8,128)} async-done(((f32[4096,1024]{0,1:T(8,128)}), f32[256,1024]{0,1:T(8,128)}) %reduce-scatter.6.cloned.1.call-update) | async-done | bytes 1048592 | tf_op jit(solution)/shard_map/reduce_scatter | solution.py:14
  352.6 16.9 %fusion = f32[2048,1024]{1,0:T(8,128)} fusion(f32[256,1024]{0,1:T(8,128)} %reduce-scatter.6.cloned.1.call-done, f32[256,4096]{1,0:T(8,128)} %all-gather.6.cloned.1.call-done, s32[]{:T(128)S(6)} %select_n.37), kind=kOutput, calls=%fused_computation.1 | convolution fusion | flops 6442450944 | bytes 11534340 | tf_op jit(solution)/shard_map/dot_general | solution.py:66
  369.6 0.9 copy-done.2
  370.5 0.1 select_reduce_fusion
  370.6 80.9 %reduce-scatter.4.cloned.1.call-done = f32[256,512]{1,0:T(8,128)} async-done(((f32[4096,512]{1,0:T(8,128)}), f32[256,512]{1,0:T(8,128)}) %reduce-scatter.4.cloned.1.call-update) | async-done | bytes 524304 | tf_op jit(solution)/shard_map/reduce_scatter | solution.py:14
  451.5 1.9 multiply_reduce_fusion.2
  453.4 1.2 fusion.11
  454.6 2.5 copy.13
  457.1 50.8 %all-gather.8.cloned.1.call-done = f32[128,4096]{1,0:T(8,128)} async-done(((f32[128,512]{1,0:T(8,128)}), f32[128,4096]{1,0:T(8,128)}) %all-gather.8.cloned.1.call-update) | async-done | bytes 2097168 | tf_op jit(solution)/shard_map/all_gather | solution.py:45
  507.9 96.6 %reduce-scatter.8.cloned.1.call-done = f32[128,1024]{1,0:T(8,128)} async-done(((f32[2048,1024]{1,0:T(8,128)}), f32[128,1024]{1,0:T(8,128)}) %reduce-scatter.8.cloned.1.call-update) | async-done | bytes 524304 | tf_op jit(solution)/shard_map/reduce_scatter | solution.py:65
  604.5 9.3 %fusion.12 = (f32[128,1024]{1,0:T(8,128)}, f32[1024]{0:T(1024)S(1)}) fusion(f32[2048,1024]{1,0:T(8,128)} %param.11, s32[]{:T(128)S(6)} %select_n.38, f32[128,1024]{1,0:T(8,128)} %reduce-scatter.8.cloned.1.call-done, f32[128,4096]{1,0:T(8,128)} %all-gather.8.cloned.1.call-done, s32[]{:T(128)S(6)} %select_n.37), kind=kOutput, calls=%fused_computation.20 | convolution fusion | flops 3221748736 | bytes 11014152 | tf_op jit(solution)/shard_map/dot_general | solution.py:61
  613.8 29.8 %all-reduce = (f32[512]{0:T(512)}, f32[1024]{0:T(1024)S(1)}) all-reduce(f32[512]{0:T(512)S(1)} %add.63, f32[1024]{0:T(1024)S(1)} %add.68), channel_id=1, replica_groups=mesh['leaf'=8,'grid'=16] {'grid'}, use_global_device_ids=true, to_apply=%region_3.4 | all-reduce | flops 1536 | bytes 12288 | tf_op jit(solution)/shard_map/psum | solution.py:90
  643.7 0.6 add.69
  (12 shorter events, 0.1 us)
Async XLA Ops:
  7.2 77.6 %all-gather.6.cloned.1.call-start = ((), (), s32[]{:S(2)}) async-start(), calls=%async_computation.5 | async-start | bytes 4718592 | tf_op jit(solution)/shard_map/all_gather | solution.py:44
  7.9 148.5 %all-gather.4.cloned.1.call-start = ((), (), s32[]{:S(2)}) async-start(), calls=%async_computation.3 | async-start | bytes 4718592 | tf_op jit(solution)/shard_map/all_gather | solution.py:43
  8.6 344.0 %reduce-scatter.6.cloned.1.call-start = ((), (), s32[]{:S(2)}) async-start(), calls=%async_computation.6 | async-start | bytes 17825792 | tf_op jit(solution)/shard_map/reduce_scatter | solution.py:14
  173.6 1.0 copy-start
  173.7 277.9 %reduce-scatter.4.cloned.1.call-start = ((), (), s32[]{:S(2)}) async-start(), calls=%async_computation.4 | async-start | bytes 8912896 | tf_op jit(solution)/shard_map/reduce_scatter | solution.py:14
  185.2 322.7 %all-gather.8.cloned.1.call-start = ((), (), s32[]{:S(2)}) async-start(), calls=%async_computation.7 | async-start | bytes 2359296 | tf_op jit(solution)/shard_map/all_gather | solution.py:45
  185.8 418.7 %reduce-scatter.8.cloned.1.call-start = ((), (), s32[]{:S(2)}) async-start(), calls=%async_computation.8 | async-start | bytes 8912896 | tf_op jit(solution)/shard_map/reduce_scatter | solution.py:65
  369.5 1.0 copy-start.2
  369.5 83.9 %copy-start.1 = (f32[256,1024]{0,1:T(8,128)S(1)}, f32[256,1024]{0,1:T(8,128)}, u32[]{:S(2)}) copy-start(f32[256,1024]{0,1:T(8,128)} %reduce-scatter.6.cloned.1.call-done) | copy-start | bytes 3145732
  457.1 186.5 %copy-start.3 = (f32[1024]{0:T(1024)S(1)}, f32[1024]{0:T(1024)}, u32[]{:S(2)}) copy-start(f32[1024]{0:T(1024)} %param.13) | copy-start | bytes 12292
Sparse Core Ops, SparseCore 0:
  10.3 74.3 all-gather.5
  87.0 69.3 all-gather.3
  173.8 178.8 reduce-scatter.5
  354.9 96.5 reduce-scatter.3
  453.7 54.1 all-gather.7
  510.2 94.2 reduce-scatter.7
where the time goes:
time: 651 us
  waiting for transfers between devices  526 us (81%)
  matrix products  70.2 us (11%)
  blocking collectives  29.8 us (5%)
  between operations  14.2 us (2%)
    reduce_scatter x2, waiting for transfers between devices, root_times(): lax.psum_scatter(lax.dot_general(root_rows, panel, (((0,), (0,)), ((), ()...  248 us
    reduce_scatter x1, waiting for transfers between devices, local(): lax.psum_scatter(lax.dot_general(middle_rows, root_side, (((0,), (0,)), (...  96.6 us
    all_gather x1, waiting for transfers between devices, local(): lax.all_gather(middle_panel, 'leaf', axis=1, tiled=True)  73.6 us
    all_gather x1, waiting for transfers between devices, local(): lax.all_gather(root_inverse, 'leaf', axis=1, tiled=True)  55.4 us
    all_gather x1, waiting for transfers between devices, local(): lax.all_gather(middle_inverse, 'leaf', axis=1, tiled=True)  50.8 us
    psum x1, blocking collectives, local(): middle_total, lower_total = lax.psum((middle_part, lower_part), 'grid')  29.8 us
    dot_general x2, matrix products, root_times(): lax.dot_general(root_rows, panel, (((0,), (0,)), ((), ())), precision=exa...  27.7 us
    dot_general x1, matrix products, local(): lax.dot_general(middle_rows, root_side, (((0,), (0,)), ((), ())), precisi...  16.9 us
  transfers between devices with their start and end apart: 6, of which 6 were waited for; matrix products, arithmetic and copies ran while one was open for 8% of the time, Pallas kernels for 0%

commit v1 on v0

v1 whole, which is shorter than its diff:
```python
import functools

import jax
import jax.numpy as jnp
from jax import lax
from jax.experimental import pallas as pl
from jax.experimental.pallas import tpu as pltpu
from jax.sharding import PartitionSpec as P

MESH = pl.DeviceIdType.MESH
F32 = jnp.float32
BF16 = jnp.bfloat16
MIB = 2**20


def device(z, a, y, b, c):
    return (z * 2 + a, y * 4 + b * 2 + c)


def flip(v, k):
    if k == 0:
        return v
    if k == 1:
        return v + 1 - 2 * (v % 2)
    if k == 2:
        return (v + 2) % 4
    return 3 - v


def high_low(x):
    high = x.astype(BF16)
    low = (x - high.astype(F32)).astype(BF16)
    return high, low


def kernel(
    s_hbm, minv_hbm, p_hbm, l_hbm, m_hbm, pattern, diag_ref,
    f_out, mid_out, root_out, par_out, low_out,
    s_buf, p_col, red, p_row, m_row, ft, f_part, ft_src, f_recv, r_part, r_recv, q_part, q_recv,
    m_stage, l_own, m_own, mm, red_acc, sums,
    s_split, red_hi, red_lo, b_hi, b_lo, pc_hi, pc_lo, a_tmp, q_tmp,
    loc, mst, prow_s, prow_r, mrow_s, mrow_r, pc_s, pc_r, pcs_s, pcs_r, x_s, x_r, z_s, z_r,
    red_s, red_r, reds_s, reds_r, fx_s, fx_r, ft_s, ft_r, rx_s, rx_r, qx_s, qx_r, sum_s, sum_r,
):
    leaf = lax.axis_index("leaf")
    grid = lax.axis_index("grid")
    z, a = leaf // 2, leaf % 2
    y, b, c = grid // 4, (grid // 2) % 2, grid % 2
    front, idx = z // 2, leaf % 4
    same = a == b
    here_rows = pl.ds(pl.multiple_of(c * 256, 256), 256)
    sib_rows = pl.ds(pl.multiple_of((1 - c) * 256, 256), 256)

    def at_idx(i):
        return (front * 4 + i, grid)

    def at_y(k):
        return (leaf, flip(y, k) * 4 + grid % 4)

    def at_z(k):
        return (flip(z, k) * 2 + a, grid)

    sibling = (leaf, grid + 1 - 2 * c)
    partner = (leaf, y * 4 + (1 - b) * 2 + c)

    def remote(src, dst, ss, rs, dev):
        return pltpu.make_async_remote_copy(
            src_ref=src, dst_ref=dst, send_sem=ss, recv_sem=rs, device_id=dev, device_id_type=MESH
        )

    bar = pltpu.get_barrier_semaphore()

    def greet(dev):
        pl.semaphore_signal(bar, inc=1, device_id=dev, device_id_type=MESH)

    @pl.loop(1, 16)
    def _(k):
        greet((leaf, (grid + k) % 16))

    for k in range(1, 4):
        greet(at_z(k))
        greet(at_idx(flip(idx, k)))
        greet(((z * 2) + ((a * 2 + b + k) % 4) // 2, y * 4 + ((a * 2 + b + k) % 4) % 2 * 2 + c))
    on_turn = idx == y
    for yy in range(4):
        for cc in range(2):
            @pl.when(jnp.logical_not(on_turn & (yy == y) & (cc == c)))
            def _():
                greet((front * 4 + y, yy * 4 + b * 2 + cc))
    pl.semaphore_wait(bar, 15 + 9 + 8 - on_turn.astype(jnp.int32))

    prow = [None] + [
        remote(p_hbm, p_row.at[k], prow_s.at[k], prow_r.at[k], at_idx(flip(idx, k))) for k in range(1, 4)
    ]
    for k in (2, 3, 1):
        prow[k].start()
    step_one = remote(s_hbm, s_buf.at[0, pl.ds(pl.multiple_of(b * 256, 256), 256)], x_s.at[0], x_r.at[0],
                      device(z, a, y, a, c))
    step_two = remote(s_hbm, s_buf.at[0, pl.ds(pl.multiple_of(b * 256, 256), 256)], x_s.at[1], x_r.at[1],
                      device(z, 1 - a, y, a, c))
    step_out = remote(s_hbm, s_buf.at[0, pl.ds(pl.multiple_of(b * 256, 256), 256)], x_s.at[0], x_r.at[0],
                      device(z, 1 - a, y, a, c))
    own_s = pltpu.make_async_copy(s_hbm, s_buf.at[0, pl.ds(pl.multiple_of(b * 256, 256), 256)], loc.at[0])

    @pl.when(same)
    def _():
        own_s.start()
        step_out.start()

    @pl.when(jnp.logical_not(same))
    def _():
        step_one.start()
        step_two.start()

    pcol = [None] + [
        remote(p_hbm, p_col.at[k, here_rows], pc_s.at[k], pc_r.at[k], at_y(k)) for k in range(1, 4)
    ]
    for k in (1, 3, 2):
        pcol[k].start()
    own_prow = pltpu.make_async_copy(p_hbm, p_row.at[0], loc.at[1])
    own_pcol = pltpu.make_async_copy(p_hbm, p_col.at[0, here_rows], loc.at[2])
    own_mrow = pltpu.make_async_copy(minv_hbm, m_row.at[0], loc.at[3])
    own_l = pltpu.make_async_copy(l_hbm, l_own, loc.at[4])
    own_m = pltpu.make_async_copy(
        m_hbm.at[pl.ds(pl.multiple_of(grid * 128, 128), 128)], m_own, loc.at[5])
    own_prow.start()

    def m_load(k, slot):
        start = pl.multiple_of(flip(idx, k) * 512, 512)
        return pltpu.make_async_copy(m_hbm.at[pl.ds(start, 512)], m_stage.at[slot], mst.at[slot])

    m_load(0, 0).start()
    m_load(1, 1).start()
    own_l.start()
    own_pcol.start()
    own_mrow.start()
    own_m.start()
    pcs = [remote(p_hbm if k == 0 else p_col.at[k, here_rows], p_col.at[k, here_rows],
                  pcs_s.at[k], pcs_r.at[k], sibling) for k in range(4)]
    pcs[0].start()

    def split_m(slot):
        @pl.loop(0, 16)
        def _(i):
            rows = pl.ds(pl.multiple_of(i * 32, 32), 32)
            hi, lo = high_low(m_stage[slot, rows])
            b_hi[rows] = hi
            b_lo[rows] = lo

    def accumulate(acc, m, lhs, rhs_hi, rhs_lo, n, first):
        @pl.loop(0, n // 256)
        def _(j):
            cols = pl.ds(pl.multiple_of(j * 256, 256), 256)
            hi = rhs_hi[:, cols]
            part = jnp.dot(lhs[0:m], hi, preferred_element_type=F32)
            part += jnp.dot(lhs[m:2 * m], hi, preferred_element_type=F32)
            part += jnp.dot(lhs[0:m], rhs_lo[:, cols], preferred_element_type=F32)
            if first:
                acc[:, cols] = part
            else:
                acc[:, cols] += part

    zs = [None] + [
        remote(s_buf.at[0], s_buf.at[k], z_s.at[k], z_r.at[k], at_z(k)) for k in range(1, 4)
    ]

    mrow = [None] + [
        remote(minv_hbm, m_row.at[k], mrow_s.at[k], mrow_r.at[k], at_idx(flip(idx, k))) for k in range(1, 4)
    ]

    for k in range(4):
        if k == 0:
            own_prow.wait()
        else:
            prow[k].wait_recv()
        m_load(k, k % 2).wait()
        split_m(k % 2)
        if k + 2 < 4:
            m_load(k + 2, k % 2).start()
        hi, lo = high_low(p_row[k])
        a_tmp[0:256] = hi
        a_tmp[256:512] = lo
        accumulate(red_acc, 256, a_tmp, b_hi, b_lo, 1024, k == 0)
        if k == 0:
            @pl.when(same)
            def _():
                own_s.wait()
                step_one.wait_recv()

            @pl.when(jnp.logical_not(same))
            def _():
                step_one.wait_recv()
                step_two.wait_recv()
            for kz in (3, 2, 1):
                zs[kz].start()
    own_l.wait()
    front_q = leaf // 2
    for i in range(2):
        keep = pattern[front_q, grid * 2 + i].astype(F32)
        rows = slice(i * 128, i * 128 + 128)
        l_own[rows] = l_own[rows] * keep
    red_acc[...] = l_own[...] - red_acc[...]
    red[0, here_rows] = red_acc[...]
    ry = [None] + [
        remote(red_acc, red.at[k, here_rows], red_s.at[k], red_r.at[k], at_y(k)) for k in range(1, 4)
    ]
    rs = [remote(red_acc if k == 0 else red.at[k, here_rows], red.at[k, here_rows],
                 reds_s.at[k], reds_r.at[k], sibling) for k in range(4)]
    for k in (1, 3, 2):
        ry[k].start()
    rs[0].start()
    for k in (2, 3, 1):
        mrow[k].start()
    for k in range(1, 4):
        pcol[k].wait_recv()
        pcs[k].start()
    own_pcol.wait()
    for k in range(4):
        pcs[k].wait_recv()

    def split_s(slot):
        @pl.loop(0, 16)
        def _(i):
            rows = pl.ds(pl.multiple_of(i * 32, 32), 32)
            hi, lo = high_low(s_buf[slot, rows])
            s_split[slot, rows] = hi
            s_split[slot, pl.ds(pl.multiple_of(512 + i * 32, 32), 32)] = lo

    for n, k in enumerate((0, 3, 1, 2)):
        if k:
            zs[k].wait_recv()
        split_s(k)
        far = flip(z, k)
        for ky in range(4):
            @pl.when(flip(y, ky) == far)
            def _():
                hi, lo = high_low(p_col[ky])
                pc_hi[...] = hi
                pc_lo[...] = lo
        accumulate(f_part, 512, s_split.at[k], pc_hi, pc_lo, 512, n == 0)
    other_rows = pl.ds(pl.multiple_of((1 - b) * 256, 256), 256)
    own_rows = pl.ds(pl.multiple_of(b * 256, 256), 256)
    fx = remote(f_part.at[other_rows], f_recv, fx_s.at[0], fx_r.at[0], partner)
    fx.start()

    def root_chunk(k, first):
        if k:
            ry[k].wait_recv()
            rs[k].start()
        rs[k].wait_recv()

        @pl.loop(0, 16)
        def _(i):
            rows = pl.ds(pl.multiple_of(i * 32, 32), 32)
            hi, lo = high_low(red[k, rows])
            red_hi[k, rows] = hi
            red_lo[k, rows] = lo

        far = flip(y, k)
        for kz in range(4):
            @pl.when(flip(z, kz) == far)
            def _():
                accumulate(r_part, 512, s_split.at[kz], red_hi.at[k], red_lo.at[k], 1024, first)

    root_chunk(0, True)

    fx.wait_recv()
    f_all = f_part[own_rows] + f_recv[...]
    f_out[...] = -f_all
    turned = f_all.T
    for cc in range(2):
        for bb in range(2):
            ft_src[cc, bb * 128:bb * 128 + 128] = turned[bb * 256 + cc * 128:bb * 256 + cc * 128 + 128]
    own_ft = pltpu.make_async_copy(ft_src.at[c], ft.at[y, c], loc.at[6])

    def ft_copy(i, cc):
        return remote(ft_src.at[cc], ft.at[y, c], ft_s.at[i, cc], ft_r.at[y, c],
                      (front * 4 + i, idx * 4 + b * 2 + cc))

    for i in range(4):
        for cc in range(2):
            mine = on_turn & (i == idx) & (cc == c)

            @pl.when(mine)
            def _():
                own_ft.start()

            @pl.when(jnp.logical_not(mine))
            def _():
                ft_copy(i, cc).start()

    own_mrow.wait()
    mid = jnp.sum(p_row[0] * f_all, axis=0, keepdims=True)
    row_at = grid * 128 + lax.broadcasted_iota(jnp.int32, (128, 512), 0)
    col_at = idx * 512 + lax.broadcasted_iota(jnp.int32, (128, 512), 1)
    mid += jnp.sum(jnp.where(row_at == col_at, m_row[0], 0.0), axis=0, keepdims=True)
    for i in range(4):
        sums[0, 8 + i:9 + i] = mid[:, i * 128:i * 128 + 128]
        sums[0, 12 + i:13 + i] = jnp.zeros((1, 128), F32)

    for k in (1, 3, 2):
        root_chunk(k, False)
    rx = remote(r_part.at[other_rows], r_recv, rx_s.at[0], rx_r.at[0], partner)
    rx.start()

    m_load(0, 0).start()
    m_load(1, 1).start()
    for k in range(4):
        if k:
            mrow[k].wait_recv()
        m_load(k, k % 2).wait()
        split_m(k % 2)
        if k + 2 < 4:
            m_load(k + 2, k % 2).start()
        hi, lo = high_low(m_row[k])
        q_tmp[0:128] = hi
        q_tmp[128:256] = lo
        accumulate(mm, 128, q_tmp, b_hi, b_lo, 1024, k == 0)

    for n, k in enumerate((0, 1, 3, 2)):
        far = flip(y, k)
        for cc in range(2):
            @pl.when(on_turn & (k == 0) & (cc == c))
            def _():
                own_ft.wait()

            @pl.when(jnp.logical_not(on_turn & (k == 0) & (cc == c)))
            def _():
                remote(ft_src.at[cc], ft.at[far, cc], ft_s.at[0, cc], ft_r.at[far, cc], partner).wait_recv()
            hi, lo = high_low(ft[far, cc])
            a_tmp[0:256, cc * 256:cc * 256 + 256] = hi
            a_tmp[256:512, cc * 256:cc * 256 + 256] = lo
        accumulate(q_part, 256, a_tmp, red_hi.at[k], red_lo.at[k], 1024, n == 0)
    qx = remote(q_part.at[pl.ds(pl.multiple_of((1 - b) * 128, 128), 128)], q_recv, qx_s.at[0], qx_r.at[0], partner)
    qx.start()

    rx.wait_recv()
    root = r_part[own_rows] + r_recv[...]
    root_out[...] = -root
    low = jnp.sum(l_own[...] * root, axis=0, keepdims=True)
    own_m.wait()
    qx.wait_recv()
    par = mm[...] - (q_part[pl.ds(pl.multiple_of(b * 128, 128), 128)] + q_recv[...])
    par_out[...] = -par
    low += jnp.sum(m_own[...] * par, axis=0, keepdims=True)
    for i in range(8):
        sums[0, i:i + 1] = low[:, i * 128:i * 128 + 128]

    def sum_copy(k):
        return remote(sums.at[0], sums.at[k], sum_s.at[k], sum_r.at[k], (leaf, (grid + k) % 16))

    for k in range(1, 16):
        sum_copy(k).start()
    total = sums[0]
    for k in range(1, 16):
        sum_copy(k).wait_recv()
    for k in range(1, 16):
        total += sums[k]
    mid_out[...] = total[8:16]
    low_out[...] = total[0:8] + diag_ref[...]

    for k in range(1, 4):
        prow[k].wait_send()
        pcol[k].wait_send()
        zs[k].wait_send()
        mrow[k].wait_send()
        ry[k].wait_send()
    for k in range(4):
        pcs[k].wait_send()
        rs[k].wait_send()

    @pl.when(same)
    def _():
        step_out.wait_send()

    @pl.when(jnp.logical_not(same))
    def _():
        step_one.wait_send()
        step_two.wait_send()
    fx.wait_send()
    rx.wait_send()
    qx.wait_send()
    for i in range(4):
        for cc in range(2):
            @pl.when(jnp.logical_not(on_turn & (i == idx) & (cc == c)))
            def _():
                ft_copy(i, cc).wait_send()
    for k in range(1, 16):
        sum_copy(k).wait_send()


def local(root_inverse, middle_inverse, middle_panel, lower_root, lower_middle, block_pattern, lower_diagonal):
    dma = pltpu.SemaphoreType.DMA
    vmem = pl.BlockSpec(memory_space=pltpu.VMEM)
    hbm = pl.BlockSpec(memory_space=pl.ANY)
    scratch = [
        pltpu.VMEM(shape, F32)
        for shape in (
            (4, 512, 512), (4, 512, 512), (4, 512, 1024), (4, 256, 512), (4, 128, 512), (4, 2, 256, 256),
            (512, 512), (2, 256, 256), (256, 512), (512, 1024), (256, 1024), (256, 1024), (128, 1024),
            (2, 512, 1024), (256, 1024), (128, 1024), (128, 1024), (256, 1024), (16, 16, 128),
        )
    ] + [
        pltpu.VMEM(shape, BF16)
        for shape in (
            (4, 1024, 512), (4, 512, 1024), (4, 512, 1024), (512, 1024), (512, 1024),
            (512, 512), (512, 512), (512, 512), (256, 512),
        )
    ] + [
        dma((7,)), dma((2,)), dma((4,)), dma((4,)), dma((4,)), dma((4,)), dma((4,)), dma((4,)), dma((4,)), dma((4,)),
        dma((2,)), dma((2,)), dma((4,)), dma((4,)),
        dma((4,)), dma((4,)), dma((4,)), dma((4,)), dma((1,)), dma((1,)), dma((4, 2)), dma((4, 2)),
        dma((1,)), dma((1,)), dma((1,)), dma((1,)), dma((16,)), dma((16,)),
    ]
    first, mid, root, par, low = pl.pallas_call(
        kernel,
        out_shape=(
            jax.ShapeDtypeStruct((256, 512), F32),
            jax.ShapeDtypeStruct((8, 128), F32),
            jax.ShapeDtypeStruct((256, 1024), F32),
            jax.ShapeDtypeStruct((128, 1024), F32),
            jax.ShapeDtypeStruct((8, 128), F32),
        ),
        in_specs=[hbm, hbm, hbm, hbm, hbm, pl.BlockSpec(memory_space=pltpu.SMEM), vmem],
        out_specs=(vmem,) * 5,
        scratch_shapes=scratch,
        compiler_params=pltpu.CompilerParams(
            collective_id=0, has_side_effects=True, vmem_limit_bytes=60 * MIB
        ),
        cost_estimate=pl.CostEstimate(flops=18 * 10**9, bytes_accessed=16 * MIB, transcendentals=0),
        name="selected_inverse",
    )(
        root_inverse, middle_inverse, middle_panel, lower_root, lower_middle, block_pattern,
        lower_diagonal.reshape(8, 128),
    )
    return first, mid.reshape(1024)[:512], root, par, low.reshape(1024)


def solution(mesh):
    in_specs = (
        P("grid", "leaf"),
        P("grid", "leaf"),
        P("grid", "leaf"),
        P("grid", "leaf"),
        P(None, "leaf"),
        P(),
        P("leaf"),
    )
    out_specs = (P("grid", "leaf"), P("leaf"), P("grid", "leaf"), P("grid", "leaf"), P("leaf"))
    return jax.shard_map(local, mesh=mesh, in_specs=in_specs, out_specs=out_specs, check_vma=False)
```

time: 651 us -> 234 us (0.36)
  waiting for transfers between devices: 526 us -> 0 us
  Pallas kernels: 0 us -> 224 us
  matrix products: 70.2 us -> 0 us
  blocking collectives: 29.8 us -> 0 us
  between operations: 14.2 us -> 0.64 us
    reduce_scatter x3 -> x0, waiting for transfers between devices: 344 us -> none  [the longest x2 248 us: root_times(): lax.psum_scatter(lax.dot_general(root_rows, panel, (((0,), (0,)), ((), ()...]
    pallas_call x0 -> x1, Pallas kernels: none -> 224 us  [local(): pl.pallas_call(kernel, out_shape=(jax.ShapeDtypeStruct((256, 512), F32),...]
    all_gather x3 -> x0, waiting for transfers between devices: 180 us -> none  [the longest x1 73.6 us: local(): lax.all_gather(middle_panel, 'leaf', axis=1, tiled=True)]
    dot_general x5 -> x0, matrix products: 70.2 us -> none  [the longest x2 27.7 us: root_times(): lax.dot_general(root_rows, panel, (((0,), (0,)), ((), ())), precision=exa...]
    psum x1 -> x0, blocking collectives: 29.8 us -> none  [local(): middle_total, lower_total = lax.psum((middle_part, lower_part), 'grid')]
  transfers between devices with their start and end apart: 6 -> 0, of which waited for: 6 -> 0; matrix products, arithmetic and copies ran while one was open for 8% -> 0% of each run, Pallas kernels for 0% -> 0%
where the time goes in v1:
time: 234 us
  Pallas kernels  224 us (96%)
  local copies, waits for them, and re-layouts  8.58 us (4%)
    pallas_call x1, Pallas kernels, local(): pl.pallas_call(kernel, out_shape=(jax.ShapeDtypeStruct((256, 512), F32),...  224 us
    unnamed x4, local copies, waits for them, and re-layouts  7.33 us

profile of v1, /device:TPU:1, one launch (start us, length us, event | category | flops | bytes accessed | tf_op | source)
XLA Modules:
  0.0 233.6 jit_solution(1399924370515569876)
XLA Ops:
  0.6 224.4 %selected_inverse.1 = (f32[256,512]{1,0:T(8,128)}, f32[8,128]{1,0:T(8,128)}, f32[256,1024]{1,0:T(8,128)}, f32[128,1024]{1,0:T(8,128)}, f32[8,128]{1,0:T(8,128)}) custom-call(f32[256,512]{1,0:T(8,128)} %s_hbm.1, f32[128,512]{1,0:T(8,128)} %minv_hbm.1, f32[256,512]{1,0:T(8,128)} %p_hbm.1, f32[256,1024]{1,0:T(8,128)} %l_hbm.1, f32[2048,1024]{1,0:T(8,128)} %m_hbm.1, ...), custom_call_target="tpu_custom_call" | custom-call | flops 17999998976 | bytes 16777216 | tf_op jit(solution)/shard_map/selected_inverse/pallas_call | solution.py:415
  225.0 1.3 slice_bitcast_fusion
  226.3 1.9 copy.16
  228.2 2.3 copy.17
  230.5 1.9 copy.18
  232.3 1.3 copy.19

commit v2 on v0

v2 whole, which is shorter than its diff:
```python
import functools

import jax
import jax.numpy as jnp
from jax import lax
from jax.experimental import pallas as pl
from jax.experimental.pallas import tpu as pltpu
from jax.sharding import PartitionSpec as P

MESH = pl.DeviceIdType.MESH
F32 = jnp.float32
BF16 = jnp.bfloat16
MIB = 2**20


def device(z, a, y, b, c):
    return (z * 2 + a, y * 4 + b * 2 + c)


def flip(v, k):
    if k == 0:
        return v
    if k == 1:
        return v + 1 - 2 * (v % 2)
    if k == 2:
        return (v + 2) % 4
    return 3 - v


def high_low(x):
    high = x.astype(BF16)
    low = (x - high.astype(F32)).astype(BF16)
    return high, low


def kernel(
    s_hbm, minv_hbm, p_hbm, l_hbm, m_hbm, pattern, diag_ref,
    f_out, mid_out, root_out, par_out, low_out,
    s_buf, p_col, l_buf, frow, ft, f_part, f_recv, r_part, r_recv, q_part, q_recv, t_part, t_recv, t_row,
    m_stage, m_own, tm, fm, sums,
    s_split, l_hi, l_lo, m_hi, m_lo, p_hi, p_lo, a_tmp, t_tmp, ft_split,
    loc, mst, x_s, x_r, z_s, z_r, py_s, py_r, ps_s, ps_r, ly_s, ly_r, ls_s, ls_r,
    fx_s, fx_r, fr_s, fr_r, ft_s, ft_r, rx_s, rx_r, qx_s, qx_r, tx_s, tx_r, tr_s, tr_r, sum_s, sum_r,
):
    leaf = lax.axis_index("leaf")
    grid = lax.axis_index("grid")
    z, a = leaf // 2, leaf % 2
    y, b, c = grid // 4, (grid // 2) % 2, grid % 2
    front, idx = z // 2, leaf % 4
    same = a == b
    differ = jnp.logical_not(same)
    here_rows = pl.ds(pl.multiple_of(c * 256, 256), 256)

    def half_rows(h):
        return pl.ds(pl.multiple_of(c * 256 + h * 128, 128), 128)

    def at_idx(k):
        return (front * 4 + flip(idx, k), grid)

    def at_y(k):
        return (leaf, flip(y, k) * 4 + grid % 4)

    def at_z(k):
        return (flip(z, k) * 2 + a, grid)

    sibling = (leaf, grid + 1 - 2 * c)
    partner = (leaf, y * 4 + (1 - b) * 2 + c)
    def remote(src, dst, ss, rs, dev):
        return pltpu.make_async_remote_copy(
            src_ref=src, dst_ref=dst, send_sem=ss, recv_sem=rs, device_id=dev, device_id_type=MESH
        )

    bar = pltpu.get_barrier_semaphore()

    def greet(dev):
        pl.semaphore_signal(bar, inc=1, device_id=dev, device_id_type=MESH)

    @pl.loop(1, 16)
    def _(k):
        greet((leaf, (grid + k) % 16))

    greet(at_z(1))
    greet(at_z(3))
    for k in range(1, 4):
        x = (a * 2 + b + k) % 4
        greet(device(z, x // 2, y, x % 2, c))
    pl.semaphore_wait(bar, 20)

    def own_s(h):
        return pltpu.make_async_copy(s_hbm.at[pl.ds(h * 128, 128)], s_buf.at[0, h, b], loc.at[h])

    def step(h, kind, n, dev):
        return remote(s_hbm.at[pl.ds(h * 128, 128)], s_buf.at[0, h, b], x_s.at[kind, h], x_r.at[n, h], dev)

    def step_one(h):
        return step(h, 0, 0, device(z, a, y, a, c))

    def step_two(h):
        return step(h, 1, 1, device(z, 1 - a, y, a, c))

    def step_out(h):
        return step(h, 0, 0, device(z, 1 - a, y, a, c))

    @pl.when(same)
    def _():
        for h in range(2):
            own_s(h).start()
            step_out(h).start()

    @pl.when(differ)
    def _():
        for h in range(2):
            step_one(h).start()
            step_two(h).start()

    own_l = pltpu.make_async_copy(l_hbm, l_buf.at[0, here_rows], loc.at[4])
    own_l.start()

    def y_own(src, buf, ss, rs, h, k):
        return remote(src, buf.at[k, half_rows(h)], ss.at[h, k], rs.at[h, k], at_y(k))

    def y_on(buf, ss, rs, h):
        came, way = (1, 3) if h == 0 else (3, 1)
        return remote(buf.at[came, half_rows(h)], buf.at[2, half_rows(h)], ss.at[h, 2], rs.at[h, 2], at_y(way))

    def p_own(h, k):
        return y_own(p_hbm.at[pl.ds(h * 128, 128)], p_col, py_s, py_r, h, k)

    def l_own(h, k):
        return y_own(l_buf.at[0, half_rows(h)], l_buf, ly_s, ly_r, h, k)

    for h, k in ((0, 1), (1, 3), (1, 1), (0, 3)):
        p_own(h, k).start()
    own_p = pltpu.make_async_copy(p_hbm, p_col.at[0, here_rows], loc.at[2])
    own_p.start()
    own_t = pltpu.make_async_copy(minv_hbm, t_row.at[0], loc.at[3])
    own_m = pltpu.make_async_copy(m_hbm.at[pl.ds(pl.multiple_of(grid * 128, 128), 128)], m_own, loc.at[5])
    own_t.start()
    own_m.start()

    def m_load(i):
        return pltpu.make_async_copy(m_hbm.at[pl.ds(i * 256, 256)], m_stage.at[i % 2], mst.at[i % 2])

    m_load(0).start()
    m_load(1).start()

    def p_side(k):
        return remote(p_hbm if k == 0 else p_col.at[k, here_rows], p_col.at[k, here_rows],
                      ps_s.at[k], ps_r.at[k], sibling)

    def l_side(k):
        return remote(l_buf.at[k, here_rows], l_buf.at[k, here_rows], ls_s.at[k], ls_r.at[k], sibling)

    p_side(0).start()

    own_l.wait()
    for i in range(2):
        keep = pattern[leaf // 2, grid * 2 + i].astype(F32)
        l_buf[0, half_rows(i)] = l_buf[0, half_rows(i)] * keep
    for h, k in ((0, 1), (1, 3), (1, 1), (0, 3)):
        l_own(h, k).start()
    l_side(0).start()

    def split_m(i):
        m_load(i).wait()

        @pl.loop(0, 8)
        def _(n):
            rows = pl.ds(pl.multiple_of(n * 32, 32), 32)
            to = pl.ds(pl.multiple_of(i % 2 * 256 + n * 32, 32), 32)
            hi, lo = high_low(m_stage[i % 2, rows])
            m_hi[i // 2, to] = hi
            m_lo[i // 2, to] = lo
        if i + 2 < 8:
            m_load(i + 2).start()

    def split_rows(src, hi_ref, lo_ref, k):
        for n, m in enumerate((0, 2, 1, 3)):
            @pl.loop(0, 4)
            def _(i):
                rows = pl.ds(pl.multiple_of(m * 128 + i * 32, 32), 32)
                to = pl.ds(pl.multiple_of(n * 128 + i * 32, 32), 32)
                hi, lo = high_low(src[k, rows])
                hi_ref[k, to] = hi
                lo_ref[k, to] = lo

    def split_s(k, h):
        for bb in range(2):
            hi, lo = high_low(s_buf[k, h, bb])
            for part, base in ((hi, 0), (lo, 256)):
                at = slice(base + bb * 128, base + bb * 128 + 128)
                for n, m in enumerate((0, 2, 1, 3)):
                    s_split[k, h, at, n * 128:n * 128 + 128] = part[:, m * 128:m * 128 + 128]

    def accumulate(acc, m, lhs, rhs_hi, rhs_lo, n, first, offset=0):
        @pl.loop(0, n // 256)
        def _(j):
            cols = pl.ds(pl.multiple_of(j * 256, 256), 256)
            from_cols = pl.ds(pl.multiple_of(offset + j * 256, 256), 256)
            hi = rhs_hi[:, from_cols]
            part = jnp.dot(lhs[0:m], hi, preferred_element_type=F32)
            part += jnp.dot(lhs[m:2 * m], hi, preferred_element_type=F32)
            part += jnp.dot(lhs[0:m], rhs_lo[:, from_cols], preferred_element_type=F32)
            if first:
                acc[:, cols] = part
            else:
                acc[:, cols] += part

    def z_own(h, bb, k):
        return remote(s_buf.at[0, h, bb], s_buf.at[k, h, bb], z_s.at[h, bb, k], z_r.at[h, bb, k], at_z(k))

    def z_on(h, bb):
        came, way = (1, 3) if bb == 0 else (3, 1)
        return remote(s_buf.at[came, h, bb], s_buf.at[2, h, bb], z_s.at[h, bb, 2], z_r.at[h, bb, 2], at_z(way))

    def s_here(h):
        @pl.when(same)
        def _():
            own_s(h).wait()
            step_one(h).wait_recv()

        @pl.when(differ)
        def _():
            step_one(h).wait_recv()
            step_two(h).wait_recv()
        for bb, k in ((0, 1), (1, 3), (1, 1), (0, 3)):
            z_own(h, bb, k).start()

    def s_on(h):
        z_own(h, 0, 1).wait_recv()
        z_on(h, 0).start()
        z_own(h, 1, 3).wait_recv()
        z_on(h, 1).start()

    def with_y(k, run):
        far = flip(z, k)
        for ky in range(4):
            @pl.when(flip(y, ky) == far)
            def _():
                run(ky)

    def f_chunk(h, k, first=False):
        split_s(k, h)

        def run(ky):
            accumulate(f_part.at[h], 256, s_split.at[k, h], p_hi.at[ky], p_lo.at[ky], 512, first)
        with_y(k, run)

    def f_near(h):
        for k, bb in ((1, 1), (3, 0)):
            z_own(h, bb, k).wait_recv()
            f_chunk(h, k)

    other_rows = pl.ds(pl.multiple_of((1 - b) * 128, 128), 128)
    own_rows = pl.ds(pl.multiple_of(b * 128, 128), 128)

    def fx(h):
        return remote(f_part.at[h, other_rows], f_recv.at[h], fx_s.at[h], fx_r.at[h], partner)

    def f_last(h):
        z_on(h, 0).wait_recv()
        z_on(h, 1).wait_recv()
        f_chunk(h, 2)
        fx(h).start()

    def fr(k, h):
        src = frow.at[1, h] if k == 3 else frow.at[0, h]
        return remote(src, frow.at[k, h], fr_s.at[k, h], fr_r.at[k, h], at_idx(1 if k == 1 else 2))

    def f_final(h):
        fx(h).wait_recv()
        whole = f_part[h, own_rows] + f_recv[h]
        for cc in range(2):
            for bb in range(2):
                at = bb * 256 + cc * 128
                frow[0, h, cc, :, bb * 128:bb * 128 + 128] = whole[:, at:at + 128]
        fr(1, h).start()
        fr(2, h).start()
        f_out[h * 128:h * 128 + 128] = -whole

    def ft_far(k, h, cc):
        return remote(frow.at[k, h, cc], ft.at[y, c, h], ft_s.at[h, k, cc], ft_r.at[h, y, c],
                      (leaf, flip(idx, k) * 4 + b * 2 + cc))

    def ft_near(k, h):
        return pltpu.make_async_copy(frow.at[k, h, c], ft.at[y, c, h], loc.at[6 + h])

    def ft_send(k, h):
        for cc in range(2):
            mine = (flip(idx, k) == y) & (c == cc)

            @pl.when(mine)
            def _():
                ft_near(k, h).start()

            @pl.when(jnp.logical_not(mine))
            def _():
                ft_far(k, h, cc).start()

    def fr_step(k, h):
        fr(k, h).wait_recv()
        if k == 1:
            fr(3, h).start()
        ft_send(k, h)

    def root_chunk(ky, first):
        far = flip(y, ky)
        for kz in range(4):
            @pl.when(flip(z, kz) == far)
            def _():
                for h in range(2):
                    accumulate(r_part.at[h], 256, s_split.at[kz, h], l_hi.at[ky], l_lo.at[ky], 1024, first)

    def l_ready(k):
        l_side(k).wait_recv()
        split_rows(l_buf, l_hi, l_lo, k)

    split_m(0)
    split_m(1)
    p_own(0, 1).wait_recv()
    y_on(p_col, py_s, py_r, 0).start()
    p_own(1, 3).wait_recv()
    y_on(p_col, py_s, py_r, 1).start()
    split_m(2)
    s_here(0)
    split_m(3)
    p_own(1, 1).wait_recv()
    p_side(1).start()
    p_own(0, 3).wait_recv()
    p_side(3).start()
    split_m(4)
    s_on(0)
    s_here(1)
    split_m(5)
    y_on(p_col, py_s, py_r, 0).wait_recv()
    y_on(p_col, py_s, py_r, 1).wait_recv()
    p_side(2).start()
    own_p.wait()
    split_m(6)
    split_m(7)
    for k in (0, 1, 3, 2):
        p_side(k).wait_recv()
        split_rows(p_col, p_hi, p_lo, k)
    f_chunk(0, 0, True)
    f_near(0)
    s_on(1)
    l_own(0, 1).wait_recv()
    y_on(l_buf, ly_s, ly_r, 0).start()
    l_own(1, 3).wait_recv()
    y_on(l_buf, ly_s, ly_r, 1).start()
    f_last(0)
    l_ready(0)
    f_chunk(1, 0, True)
    f_near(1)
    f_final(0)
    ft_send(0, 0)
    for k, h in ((1, 1), (3, 0)):
        l_own(h, k).wait_recv()
        l_side(k).start()
    f_last(1)
    fr_step(1, 0)
    fr_step(2, 0)
    root_chunk(0, True)
    f_final(1)
    ft_send(0, 1)
    y_on(l_buf, ly_s, ly_r, 0).wait_recv()
    y_on(l_buf, ly_s, ly_r, 1).wait_recv()
    l_side(2).start()
    l_ready(1)
    root_chunk(1, False)
    fr_step(3, 0)
    fr_step(1, 1)
    fr_step(2, 1)
    l_ready(3)
    root_chunk(3, False)
    fr_step(3, 1)
    l_ready(2)
    root_chunk(2, False)

    def rx(h):
        return remote(r_part.at[h, other_rows], r_recv.at[h], rx_s.at[h], rx_r.at[h], partner)

    for h in range(2):
        rx(h).start()

    tx = remote(t_part.at[other_rows], t_recv, tx_s.at[0], tx_r.at[0], partner)

    def tr(k):
        return remote(t_row.at[1] if k == 3 else t_row.at[0], t_row.at[k], tr_s.at[k], tr_r.at[k],
                      at_idx(1 if k == 1 else 2))

    def t_chunk(h, k, first):
        far = flip(y, k)
        for cc in range(2):
            came = remote(frow.at[0, h, cc], ft.at[far, cc, h], ft_s.at[h, 0, cc], ft_r.at[h, far, cc], sibling)
            if k == 0:
                @pl.when(c == cc)
                def _():
                    ft_near(0, h).wait()

                @pl.when(c != cc)
                def _():
                    came.wait_recv()
            else:
                came.wait_recv()
            hi, lo = high_low(ft[far, cc, h].T)
            ft_split[h, k, 0:256, cc * 128:cc * 128 + 128] = hi
            ft_split[h, k, 256:512, cc * 128:cc * 128 + 128] = lo
        rows = slice(h * 256, h * 256 + 256)
        accumulate(t_part, 256, ft_split.at[h, k], p_hi.at[k, rows], p_lo.at[k, rows], 512, first)

    def q_chunk(h, k, first):
        rows = slice(h * 256, h * 256 + 256)
        accumulate(q_part, 256, ft_split.at[h, k], l_hi.at[k, rows], l_lo.at[k, rows], 1024, first)

    for k in (0, 1, 3, 2):
        t_chunk(0, k, k == 0)

    for k in range(4):
        for h in range(2):
            for cc in range(2):
                hi, lo = high_low(frow[k, h, cc])
                for bb in range(2):
                    at = bb * 256 + cc * 128
                    part = slice(bb * 128, bb * 128 + 128)
                    a_tmp[h * 128:h * 128 + 128, at:at + 128] = hi[:, part]
                    a_tmp[256 + h * 128:256 + h * 128 + 128, at:at + 128] = lo[:, part]
        accumulate(fm, 256, a_tmp, m_hi.at[flip(idx, k)], m_lo.at[flip(idx, k)], 1024, k == 0)
    for k in (0, 1, 3, 2):
        t_chunk(1, k, False)
    tx.start()
    for h in range(2):
        for k in range(4):
            q_chunk(h, k, h + k == 0)
    own_t.wait()
    tx.wait_recv()
    t_row[0] = t_row[0] + (t_part[own_rows] + t_recv[...])
    tr(1).start()
    tr(2).start()
    qx = remote(q_part.at[other_rows], q_recv, qx_s.at[0], qx_r.at[0], partner)
    qx.start()

    row_at = grid * 128 + lax.broadcasted_iota(jnp.int32, (128, 512), 0)
    col_at = idx * 512 + lax.broadcasted_iota(jnp.int32, (128, 512), 1)
    mid = jnp.sum(jnp.where(row_at == col_at, t_row[0], 0.0), axis=0, keepdims=True)
    for i in range(4):
        sums[0, 8 + i:9 + i] = mid[:, i * 128:i * 128 + 128]
        sums[0, 12 + i:13 + i] = jnp.zeros((1, 128), F32)

    for k in range(4):
        if k:
            tr(k).wait_recv()
        if k == 1:
            tr(3).start()
        hi, lo = high_low(t_row[k])
        t_tmp[0:128] = hi
        t_tmp[128:256] = lo
        accumulate(tm, 128, t_tmp, m_hi.at[flip(idx, k)], m_lo.at[flip(idx, k)], 1024, k == 0)

    low = jnp.zeros((1, 1024), F32)
    for h in range(2):
        rx(h).wait_recv()
        rows = slice(h * 128, h * 128 + 128)
        root = r_part[h, own_rows] + r_recv[h] - fm[rows]
        root_out[rows] = -root
        low += jnp.sum(l_buf[0, half_rows(h)] * root, axis=0, keepdims=True)
    own_m.wait()
    qx.wait_recv()
    par = tm[...] - (q_part[own_rows] + q_recv[...])
    par_out[...] = -par
    low += jnp.sum(m_own[...] * par, axis=0, keepdims=True)
    for i in range(8):
        sums[0, i:i + 1] = low[:, i * 128:i * 128 + 128]

    def sum_copy(k):
        return remote(sums.at[0], sums.at[k], sum_s.at[k], sum_r.at[k], (leaf, (grid + k) % 16))

    for k in range(1, 16):
        sum_copy(k).start()
    total = sums[0]
    for k in range(1, 16):
        sum_copy(k).wait_recv()
    for k in range(1, 16):
        total += sums[k]
    mid_out[...] = total[8:16]
    low_out[...] = total[0:8] + diag_ref[...]

    @pl.when(same)
    def _():
        for h in range(2):
            step_out(h).wait_send()

    @pl.when(differ)
    def _():
        for h in range(2):
            step_one(h).wait_send()
            step_two(h).wait_send()
    for h in range(2):
        for k in (1, 3):
            p_own(h, k).wait_send()
            l_own(h, k).wait_send()
            for bb in range(2):
                z_own(h, bb, k).wait_send()
        y_on(p_col, py_s, py_r, h).wait_send()
        y_on(l_buf, ly_s, ly_r, h).wait_send()
        for bb in range(2):
            z_on(h, bb).wait_send()
    for k in range(4):
        p_side(k).wait_send()
        l_side(k).wait_send()
    for h in range(2):
        fx(h).wait_send()
        rx(h).wait_send()
        for k in range(4):
            if k:
                fr(k, h).wait_send()
            for cc in range(2):
                @pl.when(jnp.logical_not((flip(idx, k) == y) & (c == cc)))
                def _():
                    ft_far(k, h, cc).wait_send()
    tx.wait_send()
    for k in range(1, 4):
        tr(k).wait_send()
    qx.wait_send()
    for k in range(1, 16):
        sum_copy(k).wait_send()


def local(root_inverse, middle_inverse, middle_panel, lower_root, lower_middle, block_pattern, lower_diagonal):
    dma = pltpu.SemaphoreType.DMA
    vmem = pl.BlockSpec(memory_space=pltpu.VMEM)
    hbm = pl.BlockSpec(memory_space=pl.ANY)
    scratch = [
        pltpu.VMEM(shape, F32)
        for shape in (
            (4, 2, 2, 128, 512), (4, 512, 512), (4, 512, 1024), (4, 2, 2, 128, 256), (4, 2, 2, 128, 256),
            (2, 256, 512), (2, 128, 512), (2, 256, 1024), (2, 128, 1024), (256, 1024), (128, 1024),
            (256, 512), (128, 512), (4, 128, 512),
            (2, 256, 1024), (128, 1024), (128, 1024), (256, 1024), (16, 16, 128),
        )
    ] + [
        pltpu.VMEM(shape, BF16)
        for shape in (
            (4, 2, 512, 512), (4, 512, 1024), (4, 512, 1024), (4, 512, 1024), (4, 512, 1024),
            (4, 512, 512), (4, 512, 512), (512, 512), (256, 512), (2, 4, 512, 256),
        )
    ] + [
        dma(shape)
        for shape in (
            (8,), (2,), (2, 2), (2, 2), (2, 2, 4), (2, 2, 4), (2, 4), (2, 4), (4,), (4,), (2, 4), (2, 4), (4,), (4,),
            (2,), (2,), (4, 2), (4, 2), (2, 4, 2), (2, 4, 2), (2,), (2,), (1,), (1,), (1,), (1,), (4,), (4,),
            (16,), (16,),
        )
    ]
    first, mid, root, par, low = pl.pallas_call(
        kernel,
        out_shape=(
            jax.ShapeDtypeStruct((256, 512), F32),
            jax.ShapeDtypeStruct((8, 128), F32),
            jax.ShapeDtypeStruct((256, 1024), F32),
            jax.ShapeDtypeStruct((128, 1024), F32),
            jax.ShapeDtypeStruct((8, 128), F32),
        ),
        in_specs=[hbm, hbm, hbm, hbm, hbm, pl.BlockSpec(memory_space=pltpu.SMEM), vmem],
        out_specs=(vmem,) * 5,
        scratch_shapes=scratch,
        compiler_params=pltpu.CompilerParams(
            collective_id=0, has_side_effects=True, vmem_limit_bytes=62 * MIB
        ),
        cost_estimate=pl.CostEstimate(flops=20 * 10**9, bytes_accessed=16 * MIB, transcendentals=0),
        name="selected_inverse",
    )(
        root_inverse, middle_inverse, middle_panel, lower_root, lower_middle, block_pattern,
        lower_diagonal.reshape(8, 128),
    )
    return first, mid.reshape(1024)[:512], root, par, low.reshape(1024)


def solution(mesh):
    in_specs = (
        P("grid", "leaf"),
        P("grid", "leaf"),
        P("grid", "leaf"),
        P("grid", "leaf"),
        P(None, "leaf"),
        P(),
        P("leaf"),
    )
    out_specs = (P("grid", "leaf"), P("leaf"), P("grid", "leaf"), P("grid", "leaf"), P("leaf"))
    return jax.shard_map(local, mesh=mesh, in_specs=in_specs, out_specs=out_specs, check_vma=False)
```

time: 651 us -> 158 us (0.24)
  waiting for transfers between devices: 526 us -> 0 us
  Pallas kernels: 0 us -> 148 us
  matrix products: 70.2 us -> 0 us
  blocking collectives: 29.8 us -> 0 us
  between operations: 14.2 us -> 0.64 us
    reduce_scatter x3 -> x0, waiting for transfers between devices: 344 us -> none  [the longest x2 248 us: root_times(): lax.psum_scatter(lax.dot_general(root_rows, panel, (((0,), (0,)), ((), ()...]
    all_gather x3 -> x0, waiting for transfers between devices: 180 us -> none  [the longest x1 73.6 us: local(): lax.all_gather(middle_panel, 'leaf', axis=1, tiled=True)]
    pallas_call x0 -> x1, Pallas kernels: none -> 148 us  [local(): pl.pallas_call(kernel, out_shape=(jax.ShapeDtypeStruct((256, 512), F32),...]
    dot_general x5 -> x0, matrix products: 70.2 us -> none  [the longest x2 27.7 us: root_times(): lax.dot_general(root_rows, panel, (((0,), (0,)), ((), ())), precision=exa...]
    psum x1 -> x0, blocking collectives: 29.8 us -> none  [local(): middle_total, lower_total = lax.psum((middle_part, lower_part), 'grid')]
  transfers between devices with their start and end apart: 6 -> 0, of which waited for: 6 -> 0; matrix products, arithmetic and copies ran while one was open for 8% -> 0% of each run, Pallas kernels for 0% -> 0%
where the time goes in v2:
time: 158 us; the launch traced here: 157 us
  Pallas kernels  148 us (94%)
  local copies, waits for them, and re-layouts  8.58 us (5%)
    pallas_call x1, Pallas kernels, local(): pl.pallas_call(kernel, out_shape=(jax.ShapeDtypeStruct((256, 512), F32),...  148 us
    unnamed x4, local copies, waits for them, and re-layouts  7.33 us

profile of v2, /device:TPU:1, one launch (start us, length us, event | category | flops | bytes accessed | tf_op | source)
XLA Modules:
  0.0 157.4 jit_solution(16460983437486393981)
XLA Ops:
  0.6 148.2 %selected_inverse.1 = (f32[256,512]{1,0:T(8,128)}, f32[8,128]{1,0:T(8,128)}, f32[256,1024]{1,0:T(8,128)}, f32[128,1024]{1,0:T(8,128)}, f32[8,128]{1,0:T(8,128)}) custom-call(f32[256,512]{1,0:T(8,128)} %s_hbm.1, f32[128,512]{1,0:T(8,128)} %minv_hbm.1, f32[256,512]{1,0:T(8,128)} %p_hbm.1, f32[256,1024]{1,0:T(8,128)} %l_hbm.1, f32[2048,1024]{1,0:T(8,128)} %m_hbm.1, ...), custom_call_target="tpu_custom_call" | custom-call | flops 20000000000 | bytes 16777216 | tf_op jit(solution)/shard_map/selected_inverse/pallas_call | solution.py:555
  148.8 1.3 slice_bitcast_fusion
  150.1 1.9 %copy.16 = f32[256,512]{1,0:T(8,128)} copy(f32[256,512]{1,0:T(8,128)} %get-tuple-element.20) | data formatting | bytes 1048576
  151.9 2.3 %copy.17 = f32[256,1024]{1,0:T(8,128)} copy(f32[256,1024]{1,0:T(8,128)} %get-tuple-element.22) | data formatting | bytes 2097152
  154.2 1.9 %copy.18 = f32[128,1024]{1,0:T(8,128)} copy(f32[128,1024]{1,0:T(8,128)} %get-tuple-element.23) | data formatting | bytes 1048576
  156.1 1.3 copy.19
